TPU v7x, 256 devices: a whole 4x4x8 slice. The times are simulated.
256 devices in a mesh: row: 16 (over y, z_lo, core), col: 16 (over z_hi, x).
Axes of the slice: x: 4, y: 4, z: 8 (z_hi: 4, z_lo: 2; z = z_hi * 2 + z_lo), core: 2. Of those that a mesh axis runs over, the one named last changes fastest.
Arguments:
- final_logits: float32 [64, 131072], P(None, ('row', 'col')), as said below
- labels: int32 [131072], P(('row', 'col')), may hold values from 0 to 63
- features: float32 [64, 131072], P(None, ('row', 'col')), may hold values from -1.25 to 1.25
- tiles: float32 [16, 16, 46, 256, 256], P('row', 'col'), may hold values from -0.078125 to 0.078125
- tile_rows: int32 [16, 16, 46], P('row', 'col'), may hold values from 0 to 31, as said below
- tile_cols: int32 [16, 16, 46], P('row', 'col'), may hold values from 0 to 31, as said below
- live: int32 [16, 16], P('row', 'col'), may hold values from 11 to 46
Outputs:
- grad_start: float32 [64, 131072], P(None, ('row', 'col'))
- teleport_grad: float32 [64, 131072], P(None, ('row', 'col'))
- head_grad: float32 [64, 64], replicated
Inputs may be any that keep to these rules, and one draw needn't show every extreme that they name: `final_logits`: entries lie within -400 to 400. `tile_rows`: within one device the slots name distinct (tile row, tile column) pairs. `tile_cols`: within one device the slots name distinct (tile row, tile column) pairs.
All inputs are finite; a program needn't handle non-finite values.
Results may differ from a plain program's by a relative error of at most 0.0003.
Values sent between devices are 32-bit elements; how exact they have to be, the bound alone decides.
A program may use at most 64 MiB of HBM per device.

v0:
```python
import jax
import jax.numpy as jnp
from jax import lax
from jax.sharding import PartitionSpec as P

STEPS = 4


def shards(final_logits, labels, features, tiles, tile_rows, tile_cols, live):
    class_count = final_logits.shape[0]
    node_count = final_logits.shape[1]
    local_tiles = tiles[0, 0]
    slot_count = local_tiles.shape[0]
    tile_size = local_tiles.shape[1]
    local_rows = tile_rows[0, 0]
    local_cols = tile_cols[0, 0]
    live_count = live[0, 0]
    row_tiles_count = lax.axis_size("col") * node_count // tile_size
    usable = jnp.arange(slot_count, dtype=jnp.int32)[:, None] < live_count
    selector = (
        (local_rows[:, None] == jnp.arange(row_tiles_count, dtype=jnp.int32)[None, :]) & usable
    ).astype(jnp.float32)
    probabilities = jax.nn.softmax(final_logits, axis=0)
    one_hot = (labels[None, :] == jnp.arange(class_count, dtype=jnp.int32)[:, None]).astype(
        jnp.float32
    )
    gradient = probabilities - one_hot
    teleport = jnp.zeros_like(gradient)
    for step in range(STEPS):
        teleport = teleport + 0.1 * gradient
        advance_gathered = lax.all_gather(gradient, "row", axis=1, tiled=True)
        width = advance_gathered.shape[0]
        blocks = advance_gathered.reshape(width, -1, tile_size)
        picked = jnp.take(blocks, local_cols, axis=1)
        products = jnp.einsum("csj,sji->csi", picked, local_tiles, precision=lax.Precision.HIGHEST)
        summed = jnp.einsum("csi,sn->cni", products, selector, precision=lax.Precision.HIGHEST)
        gradient = 0.9 * lax.psum_scatter(
            summed.reshape(width, row_tiles_count * tile_size),
            "col",
            scatter_dimension=1,
            tiled=True,
        )
    head_local = jnp.dot(features, teleport.T, precision=lax.Precision.HIGHEST)
    head_grad = lax.psum(head_local, ("row", "col"))
    return (gradient, teleport, head_grad)


def solution(mesh):
    in_specs = (
        P(None, ("row", "col")),
        P(("row", "col")),
        P(None, ("row", "col")),
        P("row", "col", None, None, None),
        P("row", "col", None),
        P("row", "col", None),
        P("row", "col"),
    )
    out_specs = (P(None, ("row", "col")), P(None, ("row", "col")), P())
    return jax.shard_map(shards, mesh=mesh, in_specs=in_specs, out_specs=out_specs, check_vma=False)
```

profile of v0, /device:TPU:1, one launch (start us, length us, event | category | flops | bytes accessed | tf_op | source)
XLA Modules:
  0.0 614.4 jit_solution(17156380425180869215)
XLA Ops:
  9.1 1.6 convert_subtract_fusion
  12.8 38.9 %all-gather.5.cloned.1.call-done = f32[64,8192]{1,0:T(8,128)} async-done(((f32[64,512]{1,0:T(8,128)}), f32[64,8192]{1,0:T(8,128)}) %all-gather.5.cloned.1.call-update) | async-done | bytes 2097168 | tf_op jit(solution)/shard_map/all_gather | solution.py:31
  51.6 1.9 copy.44
  53.5 2.4 gather_fusion
  55.9 13.3 %fusion.24 = f32[64,46,256]{2,0,1:T(8,128)S(1)} fusion(f32[1,1,46,256,256]{4,3,2,1,0:T(8,128)} %param.12, f32[46,64,256]{2,1,0:T(8,128)} %gather_fusion, pred[46]{0:T(512)(128)(4,1)S(1)} %compare_and_fusion), kind=kOutput, calls=%fused_computation.32 | convolution fusion | flops 2316009472 | bytes 18087982 | tf_op jit(solution)/shard_map/csj,sji->csi/dot_general | solution.py:35
  69.2 3.2 fusion.14
  72.4 2.5 copy.25
  75.0 86.3 %reduce-scatter.5.cloned.1.call-done = f32[64,512]{1,0:T(8,128)} async-done(((f32[64,8192]{1,0:T(8,128)}), f32[64,512]{1,0:T(8,128)}) %reduce-scatter.5.cloned.1.call-update) | async-done | bytes 131088 | tf_op jit(solution)/shard_map/reduce_scatter | solution.py:37
  161.2 1.6 broadcast_multiply_fusion.3
  163.0 36.7 %all-gather.7.cloned.1.call-done = f32[64,8192]{1,0:T(8,128)} async-done(((f32[64,512]{1,0:T(8,128)}), f32[64,8192]{1,0:T(8,128)}) %all-gather.7.cloned.1.call-update) | async-done | bytes 2097168 | tf_op jit(solution)/shard_map/all_gather | solution.py:31
  199.8 1.9 copy.43
  201.6 2.4 gather_fusion.1
  204.0 13.3 %fusion.29 = f32[64,46,256]{2,0,1:T(8,128)S(1)} fusion(f32[1,1,46,256,256]{4,3,2,1,0:T(8,128)} %param.12, f32[46,64,256]{2,1,0:T(8,128)} %gather_fusion.1, pred[46]{0:T(512)(128)(4,1)S(1)} %compare_and_fusion), kind=kOutput, calls=%fused_computation.33 | convolution fusion | flops 2316009472 | bytes 18087982 | tf_op jit(solution)/shard_map/csj,sji->csi/dot_general | solution.py:35
  217.3 3.2 fusion.12
  220.4 2.5 copy.26
  223.0 86.3 %reduce-scatter.7.cloned.1.call-done = f32[64,512]{1,0:T(8,128)} async-done(((f32[64,8192]{1,0:T(8,128)}), f32[64,512]{1,0:T(8,128)}) %reduce-scatter.7.cloned.1.call-update) | async-done | bytes 131088 | tf_op jit(solution)/shard_map/reduce_scatter | solution.py:37
  311.4 36.2 %all-gather.9.cloned.1.call-done = f32[64,8192]{1,0:T(8,128)} async-done(((f32[64,512]{1,0:T(8,128)}), f32[64,8192]{1,0:T(8,128)}) %all-gather.9.cloned.1.call-update) | async-done | bytes 2097168 | tf_op jit(solution)/shard_map/all_gather | solution.py:31
  347.6 1.9 copy.42
  349.5 2.4 gather_fusion.2
  351.9 13.3 %fusion.34 = f32[64,46,256]{2,0,1:T(8,128)S(1)} fusion(f32[1,1,46,256,256]{4,3,2,1,0:T(8,128)} %param.12, f32[46,64,256]{2,1,0:T(8,128)} %gather_fusion.2, pred[46]{0:T(512)(128)(4,1)S(1)} %compare_and_fusion), kind=kOutput, calls=%fused_computation.34 | convolution fusion | flops 2316009472 | bytes 18087982 | tf_op jit(solution)/shard_map/csj,sji->csi/dot_general | solution.py:35
  365.2 3.2 fusion.10
  368.4 2.5 copy.27
  371.0 86.3 %reduce-scatter.9.cloned.1.call-done = f32[64,512]{1,0:T(8,128)} async-done(((f32[64,8192]{1,0:T(8,128)}), f32[64,512]{1,0:T(8,128)}) %reduce-scatter.9.cloned.1.call-update) | async-done | bytes 131088 | tf_op jit(solution)/shard_map/reduce_scatter | solution.py:37
  457.3 1.6 multiply_add_fusion
  459.2 36.7 %all-gather.11.cloned.1.call-done = f32[64,8192]{1,0:T(8,128)} async-done(((f32[64,512]{1,0:T(8,128)}), f32[64,8192]{1,0:T(8,128)}) %all-gather.11.cloned.1.call-update) | async-done | bytes 2097168 | tf_op jit(solution)/shard_map/all_gather | solution.py:31
  495.9 1.9 copy.41
  497.8 2.4 gather_fusion.3
  500.1 13.3 %fusion.39 = f32[64,46,256]{2,0,1:T(8,128)S(1)} fusion(f32[1,1,46,256,256]{4,3,2,1,0:T(8,128)} %param.12, f32[46,64,256]{2,1,0:T(8,128)} %gather_fusion.3, pred[46]{0:T(512)(128)(4,1)S(1)} %compare_and_fusion), kind=kOutput, calls=%fused_computation.35 | convolution fusion | flops 2316009472 | bytes 18087982 | tf_op jit(solution)/shard_map/csj,sji->csi/dot_general | solution.py:35
  513.4 3.2 fusion.8
  516.6 2.5 copy.28
  519.5 77.7 %psum.7 = f32[64,64]{0,1:T(8,128)S(1)} all-reduce(f32[64,64]{0,1:T(8,128)S(1)} %convolution_bitcast_fusion), channel_id=1, replica_groups=mesh['row'=16,'col'=16] {'row','col'}, use_global_device_ids=true, to_apply=%region_6.8 | all-reduce | flops 4096 | bytes 32768 | tf_op jit(solution)/shard_map/psum | solution.py:44
  597.8 8.0 %reduce-scatter.11.cloned.1.call-done = f32[64,512]{1,0:T(8,128)} async-done(((f32[64,8192]{1,0:T(8,128)}), f32[64,512]{1,0:T(8,128)}) %reduce-scatter.11.cloned.1.call-update) | async-done | bytes 131088 | tf_op jit(solution)/shard_map/reduce_scatter | solution.py:37
  (40 shorter events, 8.6 us)
Async XLA Ops:
  7.2 512.0 %copy-start = (f32[64,512]{1,0:T(8,128)S(1)}, f32[64,512]{1,0:T(8,128)}, u32[]{:S(2)}) copy-start(f32[64,512]{1,0:T(8,128)} %param.11) | copy-start | bytes 393220
  7.2 44.5 %all-gather.5.cloned.1.call-start = ((), (), s32[]{:S(2)}) async-start(), calls=%async_computation.4 | async-start | bytes 2228224 | tf_op jit(solution)/shard_map/all_gather | solution.py:31
  10.8 150.5 %reduce-scatter.5.cloned.1.call-start = ((), (), s32[]{:S(2)}) async-start(), calls=%async_computation.5 | async-start | bytes 2228224 | tf_op jit(solution)/shard_map/reduce_scatter | solution.py:37
  55.9 13.3 %copy-start.6 = (s32[1,1,46]{2,1,0:T(1,128)S(1)}, s32[1,1,46]{2,1,0:T(1,128)}, u32[]{:S(2)}) copy-start(s32[1,1,46]{2,1,0:T(1,128)} %param.13) | copy-start | bytes 556
  74.9 124.8 %all-gather.7.cloned.1.call-start = ((), (), s32[]{:S(2)}) async-start(), calls=%async_computation.6 | async-start | bytes 2228224 | tf_op jit(solution)/shard_map/all_gather | solution.py:31
  162.8 146.5 %reduce-scatter.7.cloned.1.call-start = ((), (), s32[]{:S(2)}) async-start(), calls=%async_computation.7 | async-start | bytes 2228224 | tf_op jit(solution)/shard_map/reduce_scatter | solution.py:37
  223.0 124.7 %all-gather.9.cloned.1.call-start = ((), (), s32[]{:S(2)}) async-start(), calls=%async_computation.8 | async-start | bytes 2228224 | tf_op jit(solution)/shard_map/all_gather | solution.py:31
  311.0 146.4 %reduce-scatter.9.cloned.1.call-start = ((), (), s32[]{:S(2)}) async-start(), calls=%async_computation.9 | async-start | bytes 2228224 | tf_op jit(solution)/shard_map/reduce_scatter | solution.py:37
  368.3 89.0 %copy-start.1 = (f32[64,512]{1,0:T(8,128)S(1)}, f32[64,512]{1,0:T(8,128)}, u32[]{:S(2)}) copy-start(f32[64,512]{1,0:T(8,128)} %param.9) | copy-start | bytes 393220
  368.4 89.0 %copy-start.2 = (f32[64,512]{1,0:T(8,128)S(1)}, f32[64,512]{1,0:T(8,128)}, u32[]{:S(2)}) copy-start(f32[64,512]{1,0:T(8,128)} %reduce-scatter.5.cloned.1.call-done) | copy-start | bytes 393220
  368.4 89.0 %copy-start.4 = (f32[64,512]{1,0:T(8,128)S(1)}, f32[64,512]{1,0:T(8,128)}, u32[]{:S(2)}) copy-start(f32[64,512]{1,0:T(8,128)} %reduce-scatter.7.cloned.1.call-done) | copy-start | bytes 393220
  368.4 89.0 %copy-start.5 = (s32[512]{0:T(512)S(1)}, s32[512]{0:T(512)}, u32[]{:S(2)}) copy-start(s32[512]{0:T(512)} %param.10) | copy-start | bytes 6148
  370.9 125.0 %all-gather.11.cloned.1.call-start = ((), (), s32[]{:S(2)}) async-start(), calls=%async_computation.10 | async-start | bytes 2228224 | tf_op jit(solution)/shard_map/all_gather | solution.py:31
  459.0 60.2 %copy-start.3 = (f32[64,512]{1,0:T(8,128)}, f32[64,512]{1,0:T(8,128)S(1)}, u32[]{:S(2)}) copy-start(f32[64,512]{1,0:T(8,128)S(1)} %get-tuple-element.13) | copy-start | bytes 393220
  459.0 146.8 %reduce-scatter.11.cloned.1.call-start = ((), (), s32[]{:S(2)}) async-start(), calls=%async_computation.11 | async-start | bytes 2228224 | tf_op jit(solution)/shard_map/reduce_scatter | solution.py:37
Sparse Core Ops, SparseCore 0:
  10.9 40.7 all-gather.4
  75.0 86.1 reduce-scatter.4
  163.8 35.9 all-gather.6
  223.1 86.1 reduce-scatter.6
  311.6 36.0 all-gather.8
  371.1 86.2 reduce-scatter.8
  459.9 36.0 all-gather.10
  519.3 86.4 reduce-scatter.10
where the time goes:
time: 624 us; the launch traced here: 614 us
  waiting for transfers between devices  416 us (67%)
  blocking collectives  77.7 us (12%)
  matrix products  66.1 us (11%)
  local copies, waits for them, and re-layouts  27.7 us (4%)
  between operations  15.1 us (2%)
  other arithmetic  11.2 us (2%)
    reduce_scatter x4, waiting for transfers between devices, shards(): lax.psum_scatter(summed.reshape(width, row_tiles_count * tile_size), 'col...  267 us
    all_gather x4, waiting for transfers between devices, shards(): advance_gathered = lax.all_gather(gradient, 'row', axis=1, tiled=True)  148 us
    psum x1, blocking collectives, shards(): head_grad = lax.psum(head_local, ('row', 'col'))  77.7 us
    dot_general x4, matrix products, shards(): jnp.einsum('csj,sji->csi', picked, local_tiles, precision=lax.Precision.H...  53.2 us
    dot_general x4, matrix products, shards(): jnp.einsum('csi,sn->cni', products, selector, precision=lax.Precision.HIG...  12.7 us
  transfers between devices with their start and end apart: 8, of which 8 were waited for; matrix products, arithmetic and copies ran while one was open for 0% of the time, Pallas kernels for 0%

commit v1 on v0

v1 whole, which is shorter than its diff:
```python
import functools

import jax
import jax.numpy as jnp
from jax import lax
from jax.experimental import pallas as pl
from jax.experimental.pallas import tpu as pltpu
from jax.sharding import PartitionSpec as P

MESH = pl.DeviceIdType.MESH
STEPS = 4
CHUNKS = 4
LAG_X = 1
LAG_Z = 2
PIECES = 23

GATHER_ORDER = ((0, 1), (1, 0), (3, 0), (2, 0), (1, 1), (3, 1), (2, 1))


def kernel(
    order,
    logits,
    labels,
    features,
    tiles,
    grad_out,
    tele,
    head_out,
    staged,
    tiles_hi,
    tiles_lo,
    field,
    running,
    gathered,
    outgoing,
    from_x,
    partial,
    from_z,
    head_x,
    head_z,
    head_u,
    head_c,
    tile_sem,
    gs_sem,
    gr_sem,
    fs_sem,
    fr_sem,
    xs_sem,
    xr_sem,
    zs_sem,
    zr_sem,
    hs_sem,
    hr_sem,
):
    slots = tiles.shape[2]
    tile = tiles.shape[3]
    classes, width = logits.shape
    size = classes // CHUNKS
    halves = width // tile
    total = STEPS * CHUNKS
    row = lax.axis_index("row")
    col = lax.axis_index("col")
    core = lax.rem(row, 2)
    unit = row // 2
    y = unit // 2
    z_lo = lax.rem(unit, 2)
    x = lax.rem(col, 4)
    z_hi = col // 4

    def place(dy, dz):
        return lax.rem(y + dy, 4) * 2 + lax.rem(z_lo + dz, 2)

    def at_unit(dy, dz):
        return {"row": place(dy, dz) * 2 + core, "col": col}

    def at_x(dx):
        return {"row": row, "col": z_hi * 4 + lax.rem(x + dx, 4)}

    def at_z(dz):
        return {"row": row, "col": lax.rem(z_hi + dz, 4) * 4 + x}

    partner = {"row": unit * 2 + 1 - core, "col": col}

    def remote(src, dst, send, recv, device):
        return pltpu.make_async_remote_copy(
            src_ref=src,
            dst_ref=dst,
            send_sem=send,
            recv_sem=recv,
            device_id=device,
            device_id_type=MESH,
        )

    per_piece = slots // PIECES

    def load_piece(i):
        part = pl.ds(i * per_piece, per_piece)
        return pltpu.make_async_copy(tiles.at[0, 0, part], staged.at[part], tile_sem.at[i])

    def start_piece(i, carry):
        load_piece(i).start()
        return carry

    lax.fori_loop(0, PIECES, start_piece, 0)

    barrier = pltpu.get_barrier_semaphore()
    peers = [at_unit(dy, dz) for dy, dz in GATHER_ORDER]
    peers += [at_x(d) for d in (1, 2, 3)] + [at_z(d) for d in (1, 2, 3)] + [partner]
    for device in peers:
        pl.semaphore_signal(barrier, inc=1, device_id=device, device_id_type=MESH)

    scores = logits[...]
    powers = jnp.exp(scores - jnp.max(scores, axis=0, keepdims=True))
    probabilities = powers / jnp.sum(powers, axis=0, keepdims=True)
    class_index = lax.broadcasted_iota(jnp.int32, (classes, width), 0)
    first = probabilities - (class_index == labels[...]).astype(jnp.float32)
    tele[...] = 0.1 * first
    mine = core * 8 + unit
    for q in range(CHUNKS):
        gathered[0, q, mine] = first[q * size : (q + 1) * size]
    pl.semaphore_wait(barrier, len(peers))

    def gather_copy(par, q, i):
        dy, dz = GATHER_ORDER[i]
        block = gathered.at[par, q, mine]
        return remote(block, block, gs_sem.at[q, i], gr_sem.at[par, q, i], at_unit(dy, dz))

    def hand_copy(par, q, i):
        dy, dz = (((0, 0),) + GATHER_ORDER)[i]
        slot = place(4 - dy, dz)
        block = gathered.at[par, q, core * 8 + slot]
        return remote(block, block, fs_sem.at[q, i], fr_sem.at[par, q, i], partner)

    def x_copy(par, q, d):
        return remote(
            outgoing.at[q, lax.rem(x + d, 4)],
            from_x.at[par, q, d - 1],
            xs_sem.at[q, d - 1],
            xr_sem.at[par, q, d - 1],
            at_x(d),
        )

    def z_copy(par, q, d):
        return remote(
            partial.at[q, lax.rem(z_hi + d, 4)],
            from_z.at[par, q, d - 1],
            zs_sem.at[q, d - 1],
            zr_sem.at[par, q, d - 1],
            at_z(d),
        )

    def split(i):
        step, q = i // CHUNKS, lax.rem(i, CHUNKS)
        return step, q, lax.rem(step, 2)

    def send_gather(par, q):
        for i in reversed(range(len(GATHER_ORDER))):
            gather_copy(par, q, i).start()
        hand_copy(par, q, 0).start()

    def hand_over(i):
        _, q, par = split(i)
        for n in range(len(GATHER_ORDER)):
            gather_copy(par, q, n).wait_recv()
            hand_copy(par, q, n + 1).start()
        for n in range(len(GATHER_ORDER)):
            gather_copy(par, q, n).wait_send()

    def multiply(i):
        _, q, par = split(i)
        for n in range(len(GATHER_ORDER) + 1):
            hand_copy(par, q, n).wait()
        for c in range(2):
            for u in range(8):
                for h in range(halves):
                    value = gathered[par, q, c * 8 + u, :, h * tile : (h + 1) * tile]
                    high = value.astype(jnp.bfloat16)
                    low = (value - high.astype(jnp.float32)).astype(jnp.bfloat16)
                    field[(u * 2 + c) * halves + h] = jnp.concatenate([high, low], axis=0)
        carried = jnp.zeros((size, tile), jnp.float32)
        for s in range(slots):
            slot = order[0, s]
            both = field[order[1, s]]
            by_high = jnp.dot(both, tiles_hi[slot], preferred_element_type=jnp.float32)
            by_low = jnp.dot(both[:size], tiles_lo[slot], preferred_element_type=jnp.float32)
            product = by_high[:size] + by_high[size:] + by_low
            carried = product + order[2, s].astype(jnp.float32) * carried
            running[s] = carried
        for n in range(32):
            block, h = n // halves, n % halves
            outgoing[q, block % 4, block // 4, :, h * tile : (h + 1) * tile] = running[order[3, n]]
        for d in (2, 1, 3):
            x_copy(par, q, d).start()

    def reduce_x(i):
        _, q, par = split(i)
        for d in (1, 3, 2):
            x_copy(par, q, d).wait()
        for b in range(4):
            partial[q, b] = (
                outgoing[q, x, b] + from_x[par, q, 0, b] + from_x[par, q, 2, b]
            ) + from_x[par, q, 1, b]
        for d in (2, 1, 3):
            z_copy(par, q, d).start()

    def reduce_z(i):
        step, q, par = split(i)
        for d in (1, 3, 2):
            z_copy(par, q, d).wait()
        value = 0.9 * (
            (partial[q, z_hi] + from_z[par, q, 0] + from_z[par, q, 2]) + from_z[par, q, 1]
        )
        rows = pl.ds(pl.multiple_of(q * size, size), size)

        @pl.when(step < STEPS - 1)
        def _():
            gathered[1 - par, q, mine] = value
            send_gather(1 - par, q)
            tele[rows] = tele[rows] + 0.1 * value

        @pl.when(step == STEPS - 1)
        def _():
            grad_out[rows] = value

    def head_copies(stage):
        if stage == 0:
            return [
                remote(head_x.at[x], head_x.at[x], hs_sem.at[d - 1], hr_sem.at[d - 1], at_x(d))
                for d in (2, 1, 3)
            ]
        if stage == 1:
            return [
                remote(
                    head_z.at[z_hi], head_z.at[z_hi], hs_sem.at[d + 2], hr_sem.at[d + 2], at_z(d)
                )
                for d in (2, 1, 3)
            ]
        if stage == 2:
            return [
                remote(
                    head_u.at[unit],
                    head_u.at[unit],
                    hs_sem.at[6 + i],
                    hr_sem.at[6 + i],
                    at_unit(*GATHER_ORDER[i]),
                )
                for i in range(len(GATHER_ORDER))
            ]
        return [remote(head_c.at[core], head_c.at[core], hs_sem.at[13], hr_sem.at[13], partner)]

    def head_stage(stage):
        if stage == 0:
            value = lax.dot_general(
                features[...],
                tele[...],
                (((1,), (1,)), ((), ())),
                precision=lax.Precision.HIGHEST,
                preferred_element_type=jnp.float32,
            )
        else:
            for copy in head_copies(stage - 1):
                copy.wait()
            source = (head_x, head_z, head_u, head_c)[stage - 1]
            value = source[0]
            for n in range(1, source.shape[0]):
                value = value + source[n]
        if stage == 0:
            head_x[x] = value
        elif stage == 1:
            head_z[z_hi] = value
        elif stage == 2:
            head_u[unit] = value
        elif stage == 3:
            head_c[core] = value
        else:
            head_out[...] = value
        if stage < 4:
            for copy in head_copies(stage):
                copy.start()

    for q in range(CHUNKS):
        send_gather(0, q)

    def convert_piece(i, carry):
        load_piece(i).wait()
        for n in range(per_piece):
            value = staged[i * per_piece + n]
            high = value.astype(jnp.bfloat16)
            tiles_hi[i * per_piece + n] = high
            tiles_lo[i * per_piece + n] = (value - high.astype(jnp.float32)).astype(jnp.bfloat16)
        return carry

    lax.fori_loop(0, PIECES, convert_piece, 0)
    running[slots] = jnp.zeros((size, tile), jnp.float32)
    hand_over(0)

    head_from = (STEPS - 1) * CHUNKS - 1 + LAG_Z

    def turn(j, carry):
        @pl.when(j < total)
        def _():
            multiply(j)

        @pl.when((j >= LAG_X) & (j < total + LAG_X))
        def _():
            reduce_x(j - LAG_X)

        @pl.when(j >= LAG_Z)
        def _():
            reduce_z(j - LAG_Z)

        @pl.when(j + 1 < total)
        def _():
            hand_over(j + 1)

        for stage in range(5):

            @pl.when(j == head_from + stage)
            def _():
                head_stage(stage)

        return carry

    lax.fori_loop(0, total + LAG_Z, turn, 0)


def slot_order(tile_rows, tile_cols, live, row_count):
    slots = tile_rows.shape[0]
    index = jnp.arange(slots, dtype=jnp.int32)
    key = jnp.where(index < live, tile_rows, row_count)
    before = (key[None, :] < key[:, None]) | (
        (key[None, :] == key[:, None]) & (index[None, :] < index[:, None])
    )
    rank = jnp.sum(before.astype(jnp.int32), axis=1)
    chosen = rank[None, :] == index[:, None]
    slot = jnp.sum(jnp.where(chosen, index[None, :], 0), axis=1)
    column = jnp.sum(jnp.where(chosen, tile_cols[None, :], 0), axis=1)
    row = jnp.sum(jnp.where(chosen, key[None, :], 0), axis=1)
    keep = jnp.concatenate([jnp.zeros((1,), jnp.int32), (row[1:] == row[:-1]).astype(jnp.int32)])
    rows = jnp.arange(row_count, dtype=jnp.int32)
    upto = jnp.sum((key[None, :] <= rows[:, None]).astype(jnp.int32), axis=1)
    some = jnp.any(key[None, :] == rows[:, None], axis=1)
    last = jnp.where(some, upto - 1, slots)
    last = jnp.concatenate([last, jnp.full((slots - row_count,), slots, jnp.int32)])
    return jnp.stack([slot, column, keep, last])


def shards(final_logits, labels, features, tiles, tile_rows, tile_cols, live):
    classes, width = final_logits.shape
    units = features.shape[0]
    slots, tile = tiles.shape[2], tiles.shape[3]
    size = classes // CHUNKS
    row_count = 16 * width // tile
    order = slot_order(tile_rows[0, 0], tile_cols[0, 0], live[0, 0], row_count)
    f32 = jnp.float32
    vmem = pl.BlockSpec(memory_space=pltpu.VMEM)
    dma = pltpu.SemaphoreType.DMA
    return pl.pallas_call(
        kernel,
        out_shape=(
            jax.ShapeDtypeStruct((classes, width), f32),
            jax.ShapeDtypeStruct((classes, width), f32),
            jax.ShapeDtypeStruct((units, classes), f32),
        ),
        in_specs=[
            pl.BlockSpec(memory_space=pltpu.SMEM),
            vmem,
            vmem,
            vmem,
            pl.BlockSpec(memory_space=pl.ANY),
        ],
        out_specs=(vmem, vmem, vmem),
        scratch_shapes=[
            pltpu.VMEM((slots, tile, tile), f32),
            pltpu.VMEM((slots, tile, tile), jnp.bfloat16),
            pltpu.VMEM((slots, tile, tile), jnp.bfloat16),
            pltpu.VMEM((row_count, 2 * size, tile), jnp.bfloat16),
            pltpu.VMEM((slots + 1, size, tile), f32),
            pltpu.VMEM((2, CHUNKS, 16, size, width), f32),
            pltpu.VMEM((CHUNKS, 4, 4, size, width), f32),
            pltpu.VMEM((2, CHUNKS, 3, 4, size, width), f32),
            pltpu.VMEM((CHUNKS, 4, size, width), f32),
            pltpu.VMEM((2, CHUNKS, 3, size, width), f32),
            pltpu.VMEM((4, units, classes), f32),
            pltpu.VMEM((4, units, classes), f32),
            pltpu.VMEM((8, units, classes), f32),
            pltpu.VMEM((2, units, classes), f32),
            dma((PIECES,)),
            dma((CHUNKS, 7)),
            dma((2, CHUNKS, 7)),
            dma((CHUNKS, 8)),
            dma((2, CHUNKS, 8)),
            dma((CHUNKS, 3)),
            dma((2, CHUNKS, 3)),
            dma((CHUNKS, 3)),
            dma((2, CHUNKS, 3)),
            dma((14,)),
            dma((14,)),
        ],
        compiler_params=pltpu.CompilerParams(
            collective_id=0, has_side_effects=True, vmem_limit_bytes=56 * 2**20
        ),
        cost_estimate=pl.CostEstimate(
            flops=3 * 2 * STEPS * slots * classes * tile * tile,
            bytes_accessed=slots * tile * tile * 4,
            transcendentals=classes * width,
        ),
    )(order, final_logits, labels.reshape(1, width), features, tiles)


def solution(mesh):
    in_specs = (
        P(None, ("row", "col")),
        P(("row", "col")),
        P(None, ("row", "col")),
        P("row", "col", None, None, None),
        P("row", "col", None),
        P("row", "col", None),
        P("row", "col"),
    )
    out_specs = (P(None, ("row", "col")), P(None, ("row", "col")), P())
    return jax.shard_map(shards, mesh=mesh, in_specs=in_specs, out_specs=out_specs, check_vma=False)
```

time: 624 us -> 141 us (0.23); the launches traced: 614 us -> 141 us
  waiting for transfers between devices: 416 us -> 0 us
  Pallas kernels: 0 us -> 133 us
  blocking collectives: 77.7 us -> 0 us
  matrix products: 66.1 us -> 0 us
  local copies, waits for them, and re-layouts: 27.7 us -> 4.51 us
  between operations: 15.1 us -> 1.31 us
  other arithmetic: 11.2 us -> 2.63 us
    reduce_scatter x4 -> x0, waiting for transfers between devices: 267 us -> none  [shards(): lax.psum_scatter(summed.reshape(width, row_tiles_count * tile_size), 'col...]
    all_gather x4 -> x0, waiting for transfers between devices: 148 us -> none  [shards(): advance_gathered = lax.all_gather(gradient, 'row', axis=1, tiled=True)]
    pallas_call x0 -> x1, Pallas kernels: none -> 133 us  [shards(): pl.pallas_call(kernel, out_shape=(jax.ShapeDtypeStruct((classes, width),...]
    psum x1 -> x0, blocking collectives: 77.7 us -> none  [shards(): head_grad = lax.psum(head_local, ('row', 'col'))]
    dot_general x9 -> x0, matrix products: 66.1 us -> none  [the longest x4 53.2 us: shards(): jnp.einsum('csj,sji->csi', picked, local_tiles, precision=lax.Precision.H...]
    gather x4 -> x0, local copies, waits for them, and re-layouts: 9.41 us -> none  [shards(): picked = jnp.take(blocks, local_cols, axis=1)]
    reshape x4 -> x0, local copies, waits for them, and re-layouts: 7.43 us -> none  [shards(): blocks = advance_gathered.reshape(width, -1, tile_size)]
    unnamed x19 -> x3, local copies, waits for them, and re-layouts: 10.8 us -> 4.51 us
  transfers between devices with their start and end apart: 8 -> 0, of which waited for: 8 -> 0; matrix products, arithmetic and copies ran while one was open for 0% -> 0% of each run, Pallas kernels for 0% -> 0%
where the time goes in v1:
time: 141 us
  Pallas kernels  133 us (94%)
  local copies, waits for them, and re-layouts  4.51 us (3%)
  other arithmetic  2.63 us (2%)
    pallas_call x1, Pallas kernels, shards(): pl.pallas_call(kernel, out_shape=(jax.ShapeDtypeStruct((classes, width),...  133 us
    unnamed x3, local copies, waits for them, and re-layouts  4.51 us

profile of v1, /device:TPU:1, one launch (start us, length us, event | category | flops | bytes accessed | tf_op | source)
XLA Modules:
  0.0 141.1 jit_solution(6492637220142886650)
XLA Ops:
  1.3 0.7 compare_select_fusion
  1.9 0.1 convert_reduce_fusion.1
  2.1 0.1 fusion.2
  2.2 0.2 convert_reduce_fusion
  2.4 0.8 select_reduce_fusion.2
  3.2 0.1 slice_compare_fusion
  3.3 0.1 fusion.3
  3.3 0.6 pad_add_fusion.order
  3.9 132.7 %shard_map.94 = (f32[64,512]{1,0:T(8,128)}, f32[64,512]{1,0:T(8,128)}, f32[64,64]{1,0:T(8,128)}) custom-call(s32[4,46]{1,0:T(4,128)} %pad_add_fusion.order, f32[64,512]{1,0:T(8,128)} %logits.1, s32[1,512]{1,0:T(1,128)} %bitcast.15, f32[64,512]{1,0:T(8,128)} %features.1, f32[1,1,46,256,256]{4,3,2,1,0:T(8,128)} %tiles.1), custom_call_target="tpu_custom_call" | custom-call | flops 4630511616 | bytes 12058624 | tf_op jit(solution)/shard_map/pallas_call | solution.py:358
  136.6 1.6 %copy.14 = f32[64,512]{1,0:T(8,128)} copy(f32[64,512]{1,0:T(8,128)} %get-tuple-element.9) | data formatting | bytes 262144
  138.2 1.6 %copy.15 = f32[64,512]{1,0:T(8,128)} copy(f32[64,512]{1,0:T(8,128)} %get-tuple-element.10) | data formatting | bytes 262144
  139.7 1.4 copy.16
  (2 shorter events, 0.0 us)

commit v2 on v1

--- a/solution.py
+++ b/solution.py
@@ -13,19 +13,28 @@
 LAG_X = 1
 LAG_Z = 2
 PIECES = 23
-
-GATHER_ORDER = ((0, 1), (1, 0), (3, 0), (2, 0), (1, 1), (3, 1), (2, 1))
+DISTANCES = (2, 1, 3, 0)
+PARTS = ((0, 1), (1, 2), (3, 1))
+
+GATHER_ORDER = ((0, 1), (1, 0), (1, 1), (3, 0), (3, 1), (2, 0), (2, 1))
+HAND_AFTER = {0: 0, 2: 1, 4: 3, 6: 2}
 
 
 def kernel(
-    order,
-    logits,
+    live,
+    tile_rows,
+    tile_cols,
     labels,
-    features,
+    logits_far,
+    features_far,
     tiles,
     grad_out,
     tele,
     head_out,
+    logits,
+    features,
+    order_rows,
+    order,
     staged,
     tiles_hi,
     tiles_lo,
@@ -51,6 +60,7 @@
     zr_sem,
     hs_sem,
     hr_sem,
+    near_sem,
 ):
     slots = tiles.shape[2]
     tile = tiles.shape[3]
@@ -58,6 +68,7 @@
     size = classes // CHUNKS
     halves = width // tile
     total = STEPS * CHUNKS
+    row_tiles = 16 * halves
     row = lax.axis_index("row")
     col = lax.axis_index("col")
     core = lax.rem(row, 2)
@@ -101,7 +112,9 @@
         load_piece(i).start()
         return carry
 
-    lax.fori_loop(0, PIECES, start_piece, 0)
+    load_logits = pltpu.make_async_copy(logits_far, logits, near_sem.at[0])
+    load_features = pltpu.make_async_copy(features_far, features, near_sem.at[1])
+    load_logits.start()
 
     barrier = pltpu.get_barrier_semaphore()
     peers = [at_unit(dy, dz) for dy, dz in GATHER_ORDER]
@@ -109,6 +122,9 @@
     for device in peers:
         pl.semaphore_signal(barrier, inc=1, device_id=device, device_id_type=MESH)
 
+    lax.fori_loop(0, PIECES, start_piece, 0)
+    load_features.start()
+    load_logits.wait()
     scores = logits[...]
     powers = jnp.exp(scores - jnp.max(scores, axis=0, keepdims=True))
     probabilities = powers / jnp.sum(powers, axis=0, keepdims=True)
@@ -118,6 +134,11 @@
     mine = core * 8 + unit
     for q in range(CHUNKS):
         gathered[0, q, mine] = first[q * size : (q + 1) * size]
+    listed = slot_order(tile_rows[...], tile_cols[...], live[0, 0], row_tiles)
+    for n in range(4):
+        order_rows[n : n + 1, : listed[n].shape[1]] = listed[n]
+    load_order = pltpu.make_async_copy(order_rows, order, near_sem.at[2])
+    load_order.start()
     pl.semaphore_wait(barrier, len(peers))
 
     def gather_copy(par, q, i):
@@ -126,23 +147,28 @@
         return remote(block, block, gs_sem.at[q, i], gr_sem.at[par, q, i], at_unit(dy, dz))
 
     def hand_copy(par, q, i):
-        dy, dz = (((0, 0),) + GATHER_ORDER)[i]
-        slot = place(4 - dy, dz)
-        block = gathered.at[par, q, core * 8 + slot]
+        slot = lax.rem(y + 4 - i, 4) * 2
+        block = gathered.at[par, q, pl.ds(core * 8 + slot, 2)]
         return remote(block, block, fs_sem.at[q, i], fr_sem.at[par, q, i], partner)
 
-    def x_copy(par, q, d):
+    def z_place(block):
+        distance = lax.rem(block - z_hi + 4, 4)
+        own, two, three = (4 - distance) // 4, (distance // 2) * (3 - distance), distance // 3
+        return 1 + 2 * own - two + three
+
+    def x_copy(par, q, d, p):
+        blocks = pl.ds(*PARTS[p])
         return remote(
-            outgoing.at[q, lax.rem(x + d, 4)],
-            from_x.at[par, q, d - 1],
-            xs_sem.at[q, d - 1],
-            xr_sem.at[par, q, d - 1],
+            outgoing.at[q, lax.rem(x + d, 4), blocks],
+            from_x.at[par, q, d - 1, blocks],
+            xs_sem.at[q, d - 1, p],
+            xr_sem.at[par, q, d - 1, p],
             at_x(d),
         )
 
     def z_copy(par, q, d):
         return remote(
-            partial.at[q, lax.rem(z_hi + d, 4)],
+            partial.at[q, DISTANCES.index(d)],
             from_z.at[par, q, d - 1],
             zs_sem.at[q, d - 1],
             zr_sem.at[par, q, d - 1],
@@ -156,60 +182,69 @@
     def send_gather(par, q):
         for i in reversed(range(len(GATHER_ORDER))):
             gather_copy(par, q, i).start()
-        hand_copy(par, q, 0).start()
+
+    def fill_field(par, q, c):
+        for u in range(8):
+            for h in range(halves):
+                value = gathered[par, q, c * 8 + u, :, h * tile : (h + 1) * tile]
+                high = value.astype(jnp.bfloat16).astype(jnp.float32)
+                both = jnp.concatenate([high, value - high], axis=0)
+                field[(u * 2 + c) * halves + h] = both.astype(jnp.bfloat16)
 
     def hand_over(i):
         _, q, par = split(i)
         for n in range(len(GATHER_ORDER)):
             gather_copy(par, q, n).wait_recv()
-            hand_copy(par, q, n + 1).start()
+            if n in HAND_AFTER:
+                hand_copy(par, q, HAND_AFTER[n]).start()
+        fill_field(par, q, core)
         for n in range(len(GATHER_ORDER)):
             gather_copy(par, q, n).wait_send()
 
     def multiply(i):
         _, q, par = split(i)
-        for n in range(len(GATHER_ORDER) + 1):
+        for n in range(4):
             hand_copy(par, q, n).wait()
-        for c in range(2):
-            for u in range(8):
-                for h in range(halves):
-                    value = gathered[par, q, c * 8 + u, :, h * tile : (h + 1) * tile]
-                    high = value.astype(jnp.bfloat16)
-                    low = (value - high.astype(jnp.float32)).astype(jnp.bfloat16)
-                    field[(u * 2 + c) * halves + h] = jnp.concatenate([high, low], axis=0)
+        fill_field(par, q, 1 - core)
         carried = jnp.zeros((size, tile), jnp.float32)
         for s in range(slots):
             slot = order[0, s]
             both = field[order[1, s]]
             by_high = jnp.dot(both, tiles_hi[slot], preferred_element_type=jnp.float32)
-            by_low = jnp.dot(both[:size], tiles_lo[slot], preferred_element_type=jnp.float32)
-            product = by_high[:size] + by_high[size:] + by_low
+            if size % 16 == 0:
+                both = both[:size]
+            by_low = jnp.dot(both, tiles_lo[slot], preferred_element_type=jnp.float32)
+            product = by_high[:size] + by_high[size:] + by_low[:size]
+            if size % 16:
+                product = product + by_low[size:]
             carried = product + order[2, s].astype(jnp.float32) * carried
             running[s] = carried
-        for n in range(32):
+        for n in range(row_tiles):
             block, h = n // halves, n % halves
-            outgoing[q, block % 4, block // 4, :, h * tile : (h + 1) * tile] = running[order[3, n]]
-        for d in (2, 1, 3):
-            x_copy(par, q, d).start()
-
-    def reduce_x(i):
+            outgoing[q, block % 4, z_place(block // 4), :, h * tile : (h + 1) * tile] = running[order[3, n]]
+        for p in range(len(PARTS)):
+            for d in (2, 1, 3):
+                x_copy(par, q, d, p).start()
+
+    def reduce_x(i, p):
         _, q, par = split(i)
         for d in (1, 3, 2):
-            x_copy(par, q, d).wait()
-        for b in range(4):
+            x_copy(par, q, d, p).wait()
+        start, count = PARTS[p]
+        for b in range(start, start + count):
             partial[q, b] = (
                 outgoing[q, x, b] + from_x[par, q, 0, b] + from_x[par, q, 2, b]
             ) + from_x[par, q, 1, b]
         for d in (2, 1, 3):
-            z_copy(par, q, d).start()
+            if d in DISTANCES[start : start + count]:
+                z_copy(par, q, d).start()
 
     def reduce_z(i):
         step, q, par = split(i)
+        reduce_x(i, len(PARTS) - 1)
         for d in (1, 3, 2):
             z_copy(par, q, d).wait()
-        value = 0.9 * (
-            (partial[q, z_hi] + from_z[par, q, 0] + from_z[par, q, 2]) + from_z[par, q, 1]
-        )
+        value = 0.9 * ((partial[q, 3] + from_z[par, q, 0] + from_z[par, q, 2]) + from_z[par, q, 1])
         rows = pl.ds(pl.multiple_of(q * size, size), size)
 
         @pl.when(step < STEPS - 1)
@@ -278,8 +313,7 @@
             for copy in head_copies(stage):
                 copy.start()
 
-    for q in range(CHUNKS):
-        send_gather(0, q)
+    send_gather(0, 0)
 
     def convert_piece(i, carry):
         load_piece(i).wait()
@@ -291,8 +325,12 @@
         return carry
 
     lax.fori_loop(0, PIECES, convert_piece, 0)
+    load_order.wait()
+    load_features.wait()
     running[slots] = jnp.zeros((size, tile), jnp.float32)
     hand_over(0)
+    for q in range(1, CHUNKS):
+        send_gather(0, q)
 
     head_from = (STEPS - 1) * CHUNKS - 1 + LAG_Z
 
@@ -303,7 +341,8 @@
 
         @pl.when((j >= LAG_X) & (j < total + LAG_X))
         def _():
-            reduce_x(j - LAG_X)
+            reduce_x(j - LAG_X, 0)
+            reduce_x(j - LAG_X, 1)
 
         @pl.when(j >= LAG_Z)
         def _():
@@ -324,25 +363,40 @@
     lax.fori_loop(0, total + LAG_Z, turn, 0)
 
 
+def hand_out(*refs):
+    for source, target in zip(refs[:3], refs[3:]):
+        target[...] = source[...]
+
+
 def slot_order(tile_rows, tile_cols, live, row_count):
-    slots = tile_rows.shape[0]
-    index = jnp.arange(slots, dtype=jnp.int32)
-    key = jnp.where(index < live, tile_rows, row_count)
-    before = (key[None, :] < key[:, None]) | (
-        (key[None, :] == key[:, None]) & (index[None, :] < index[:, None])
-    )
-    rank = jnp.sum(before.astype(jnp.int32), axis=1)
-    chosen = rank[None, :] == index[:, None]
-    slot = jnp.sum(jnp.where(chosen, index[None, :], 0), axis=1)
-    column = jnp.sum(jnp.where(chosen, tile_cols[None, :], 0), axis=1)
-    row = jnp.sum(jnp.where(chosen, key[None, :], 0), axis=1)
-    keep = jnp.concatenate([jnp.zeros((1,), jnp.int32), (row[1:] == row[:-1]).astype(jnp.int32)])
-    rows = jnp.arange(row_count, dtype=jnp.int32)
-    upto = jnp.sum((key[None, :] <= rows[:, None]).astype(jnp.int32), axis=1)
-    some = jnp.any(key[None, :] == rows[:, None], axis=1)
-    last = jnp.where(some, upto - 1, slots)
-    last = jnp.concatenate([last, jnp.full((slots - row_count,), slots, jnp.int32)])
-    return jnp.stack([slot, column, keep, last])
+    slots = tile_rows.shape[1]
+
+    def index(shape, dim):
+        return lax.broadcasted_iota(jnp.int32, shape, dim)
+
+    def total(values, dim):
+        return jnp.sum(values, axis=dim, keepdims=True)
+
+    def upright(values):
+        square = (slots, slots)
+        return total(jnp.where(index(square, 0) == index(square, 1), values, 0), 1)
+
+    across = index((1, slots), 1)
+    down = index((slots, 1), 0)
+    key = jnp.where(across < live, tile_rows, row_count) * slots + across
+    key_down = upright(key)
+    rank = total(jnp.where(key < key_down, 1, 0), 1)
+    chosen = rank == across
+    slot = total(jnp.where(chosen, down, 0), 0)
+    column = total(jnp.where(chosen, upright(tile_cols), 0), 0)
+    place = index((1, 128), 1)
+    starts = place * slots
+    upto = total(jnp.where(key_down < starts + slots, 1, 0), 0)
+    below = total(jnp.where(key_down < starts, 1, 0), 0)
+    last = jnp.where(upto > below, upto - 1, slots)
+    first = total(jnp.where(chosen, total(jnp.where(key < key_down - upright(across), 1, 0), 1), 0), 0)
+    keep = jnp.where(first < across, 1, 0)
+    return slot, column, keep, last
 
 
 def shards(final_logits, labels, features, tiles, tile_rows, tile_cols, live):
@@ -351,11 +405,11 @@
     slots, tile = tiles.shape[2], tiles.shape[3]
     size = classes // CHUNKS
     row_count = 16 * width // tile
-    order = slot_order(tile_rows[0, 0], tile_cols[0, 0], live[0, 0], row_count)
     f32 = jnp.float32
     vmem = pl.BlockSpec(memory_space=pltpu.VMEM)
+    far = pl.BlockSpec(memory_space=pl.ANY)
     dma = pltpu.SemaphoreType.DMA
-    return pl.pallas_call(
+    parts = pl.pallas_call(
         kernel,
         out_shape=(
             jax.ShapeDtypeStruct((classes, width), f32),
@@ -367,10 +421,16 @@
             vmem,
             vmem,
             vmem,
-            pl.BlockSpec(memory_space=pl.ANY),
+            far,
+            far,
+            far,
         ],
         out_specs=(vmem, vmem, vmem),
         scratch_shapes=[
+            pltpu.VMEM((classes, width), f32),
+            pltpu.VMEM((units, width), f32),
+            pltpu.VMEM((4, 128), jnp.int32),
+            pltpu.SMEM((4, 128), jnp.int32),
             pltpu.VMEM((slots, tile, tile), f32),
             pltpu.VMEM((slots, tile, tile), jnp.bfloat16),
             pltpu.VMEM((slots, tile, tile), jnp.bfloat16),
@@ -388,14 +448,15 @@
             dma((PIECES,)),
             dma((CHUNKS, 7)),
             dma((2, CHUNKS, 7)),
-            dma((CHUNKS, 8)),
-            dma((2, CHUNKS, 8)),
-            dma((CHUNKS, 3)),
-            dma((2, CHUNKS, 3)),
+            dma((CHUNKS, 4)),
+            dma((2, CHUNKS, 4)),
+            dma((CHUNKS, 3, len(PARTS))),
+            dma((2, CHUNKS, 3, len(PARTS))),
             dma((CHUNKS, 3)),
             dma((2, CHUNKS, 3)),
             dma((14,)),
             dma((14,)),
+            dma((3,)),
         ],
         compiler_params=pltpu.CompilerParams(
             collective_id=0, has_side_effects=True, vmem_limit_bytes=56 * 2**20
@@ -405,7 +466,21 @@
             bytes_accessed=slots * tile * tile * 4,
             transcendentals=classes * width,
         ),
-    )(order, final_logits, labels.reshape(1, width), features, tiles)
+    )(
+        live,
+        tile_rows[0],
+        tile_cols[0],
+        labels.reshape(1, width),
+        final_logits,
+        features,
+        tiles,
+    )
+    return pl.pallas_call(
+        hand_out,
+        out_shape=tuple(jax.ShapeDtypeStruct(part.shape, f32) for part in parts),
+        in_specs=[vmem] * 3,
+        out_specs=(vmem,) * 3,
+    )(*parts)
 
 
 def solution(mesh):

time: 141 us -> 123 us (0.87)
  Pallas kernels: 133 us -> 122 us
  local copies, waits for them, and re-layouts: 4.51 us -> 0 us
  other arithmetic: 2.63 us -> 0 us
    pallas_call x1, Pallas kernels: 133 us -> 120 us  [shards(): pl.pallas_call(kernel, out_shape=(jax.ShapeDtypeStruct((classes, width),...]
    unnamed x3 -> x0, local copies, waits for them, and re-layouts: 4.51 us -> none
    pallas_call x0 -> x1, Pallas kernels: none -> 1.68 us  [shards(): pl.pallas_call(hand_out, out_shape=tuple((jax.ShapeDtypeStruct(part.shape...]
where the time goes in v2:
time: 123 us
  Pallas kernels  122 us (99%)
  between operations  1.29 us (1%)
    pallas_call x1, Pallas kernels, shards(): pl.pallas_call(kernel, out_shape=(jax.ShapeDtypeStruct((classes, width),...  120 us

profile of v2, /device:TPU:1, one launch (start us, length us, event | category | flops | bytes accessed | tf_op | source)
XLA Modules:
  0.0 123.3 jit_solution(4163126151158942878)
XLA Ops:
  1.3 120.3 %shard_map.94 = (f32[64,512]{1,0:T(8,128)}, f32[64,512]{1,0:T(8,128)}, f32[64,64]{1,0:T(8,128)}) custom-call(s32[1,1]{1,0:T(1,128)S(6)} %copy.10.live, s32[1,46]{1,0:T(1,128)} %bitcast.4, s32[1,46]{1,0:T(1,128)} %bitcast.5, s32[1,512]{1,0:T(1,128)} %bitcast.3, f32[64,512]{1,0:T(8,128)} %logits_far.1, f32[64,512]{1,0:T(8,128)} %features_far.1, ...), custom_call_target="tpu_custom_call" | custom-call | flops 4630511616 | bytes 12058624 | tf_op jit(solution)/shard_map/pallas_call | solution.py:412
  121.6 1.7 %shard_map.95 = (f32[64,512]{1,0:T(8,128)}, f32[64,512]{1,0:T(8,128)}, f32[64,64]{1,0:T(8,128)}) custom-call(f32[64,512]{1,0:T(8,128)} %get-tuple-element.6.refs_0_, f32[64,512]{1,0:T(8,128)} %get-tuple-element.7.refs_1_, f32[64,64]{1,0:T(8,128)} %get-tuple-element.8.refs_2_), custom_call_target="tpu_custom_call" | custom-call | tf_op jit(solution)/shard_map/pallas_call | solution.py:478

commit v3 on v2

--- a/solution.py
+++ b/solution.py
@@ -17,7 +17,6 @@
 PARTS = ((0, 1), (1, 2), (3, 1))
 
 GATHER_ORDER = ((0, 1), (1, 0), (1, 1), (3, 0), (3, 1), (2, 0), (2, 1))
-HAND_AFTER = {0: 0, 2: 1, 4: 3, 6: 2}
 
 
 def kernel(
@@ -90,6 +89,11 @@
     def at_z(dz):
         return {"row": row, "col": lax.rem(z_hi + dz, 4) * 4 + x}
 
+    def z_place(block):
+        distance = lax.rem(block - z_hi + 4, 4)
+        own, two, three = (4 - distance) // 4, (distance // 2) * (3 - distance), distance // 3
+        return 1 + 2 * own - two + three
+
     partner = {"row": unit * 2 + 1 - core, "col": col}
 
     def remote(src, dst, send, recv, device):
@@ -102,6 +106,9 @@
             device_id_type=MESH,
         )
 
+    def wait_bytes(ref, sem):
+        pltpu.make_async_copy(ref, ref, sem).wait()
+
     per_piece = slots // PIECES
 
     def load_piece(i):
@@ -117,8 +124,14 @@
     load_logits.start()
 
     barrier = pltpu.get_barrier_semaphore()
-    peers = [at_unit(dy, dz) for dy, dz in GATHER_ORDER]
-    peers += [at_x(d) for d in (1, 2, 3)] + [at_z(d) for d in (1, 2, 3)] + [partner]
+    unit_peers = [at_unit(dy, dz) for dy, dz in GATHER_ORDER]
+    x_peers = [at_x(d) for d in range(4)]
+    z_peers = [at_z(d) for d in range(4)]
+    x_slots = [lax.rem(x + d, 4) for d in range(4)]
+    z_slots = [z_place(block) for block in range(4)]
+    y_units = [lax.rem(y + 4 - d, 4) * 2 for d in range(4)]
+    hand_slots = [core * 8 + u for u in y_units]
+    peers = unit_peers + x_peers[1:] + z_peers[1:] + [partner]
     for device in peers:
         pl.semaphore_signal(barrier, inc=1, device_id=device, device_id_type=MESH)
 
@@ -142,37 +155,32 @@
     pl.semaphore_wait(barrier, len(peers))
 
     def gather_copy(par, q, i):
-        dy, dz = GATHER_ORDER[i]
         block = gathered.at[par, q, mine]
-        return remote(block, block, gs_sem.at[q, i], gr_sem.at[par, q, i], at_unit(dy, dz))
+        return remote(
+            block, block, gs_sem.at[q], gr_sem.at[par, q, GATHER_ORDER[i][0]], unit_peers[i]
+        )
 
     def hand_copy(par, q, i):
-        slot = lax.rem(y + 4 - i, 4) * 2
-        block = gathered.at[par, q, pl.ds(core * 8 + slot, 2)]
-        return remote(block, block, fs_sem.at[q, i], fr_sem.at[par, q, i], partner)
-
-    def z_place(block):
-        distance = lax.rem(block - z_hi + 4, 4)
-        own, two, three = (4 - distance) // 4, (distance // 2) * (3 - distance), distance // 3
-        return 1 + 2 * own - two + three
+        block = gathered.at[par, q, pl.ds(hand_slots[i], 2)]
+        return remote(block, block, fs_sem.at[q], fr_sem.at[par, q, i], partner)
 
     def x_copy(par, q, d, p):
         blocks = pl.ds(*PARTS[p])
         return remote(
-            outgoing.at[q, lax.rem(x + d, 4), blocks],
+            outgoing.at[q, x_slots[d], blocks],
             from_x.at[par, q, d - 1, blocks],
-            xs_sem.at[q, d - 1, p],
-            xr_sem.at[par, q, d - 1, p],
-            at_x(d),
+            xs_sem.at[q],
+            xr_sem.at[par, q, p],
+            x_peers[d],
         )
 
     def z_copy(par, q, d):
         return remote(
             partial.at[q, DISTANCES.index(d)],
             from_z.at[par, q, d - 1],
-            zs_sem.at[q, d - 1],
-            zr_sem.at[par, q, d - 1],
-            at_z(d),
+            zs_sem.at[q],
+            zr_sem.at[par, q],
+            z_peers[d],
         )
 
     def split(i):
@@ -183,8 +191,9 @@
         for i in reversed(range(len(GATHER_ORDER))):
             gather_copy(par, q, i).start()
 
-    def fill_field(par, q, c):
-        for u in range(8):
+    def fill_field(par, q, c, d):
+        for n in range(2):
+            u = y_units[d] + n
             for h in range(halves):
                 value = gathered[par, q, c * 8 + u, :, h * tile : (h + 1) * tile]
                 high = value.astype(jnp.bfloat16).astype(jnp.float32)
@@ -193,19 +202,19 @@
 
     def hand_over(i):
         _, q, par = split(i)
-        for n in range(len(GATHER_ORDER)):
-            gather_copy(par, q, n).wait_recv()
-            if n in HAND_AFTER:
-                hand_copy(par, q, HAND_AFTER[n]).start()
-        fill_field(par, q, core)
-        for n in range(len(GATHER_ORDER)):
-            gather_copy(par, q, n).wait_send()
+        for d in (0, 1, 3, 2):
+            blocks = pl.ds(hand_slots[0], 1 if d == 0 else 2)
+            wait_bytes(gathered.at[par, q, blocks], gr_sem.at[par, q, d])
+            hand_copy(par, q, d).start()
+            fill_field(par, q, core, d)
+        wait_bytes(gathered.at[par, q, pl.ds(core * 8, 7)], gs_sem.at[q])
 
     def multiply(i):
         _, q, par = split(i)
-        for n in range(4):
-            hand_copy(par, q, n).wait()
-        fill_field(par, q, 1 - core)
+        wait_bytes(gathered.at[par, q, pl.ds(core * 8, 8)], fs_sem.at[q])
+        for d in (0, 1, 3, 2):
+            wait_bytes(gathered.at[par, q, pl.ds(8 - core * 8, 2)], fr_sem.at[par, q, d])
+            fill_field(par, q, 1 - core, d)
         carried = jnp.zeros((size, tile), jnp.float32)
         for s in range(slots):
             slot = order[0, s]
@@ -221,16 +230,15 @@
             running[s] = carried
         for n in range(row_tiles):
             block, h = n // halves, n % halves
-            outgoing[q, block % 4, z_place(block // 4), :, h * tile : (h + 1) * tile] = running[order[3, n]]
+            outgoing[q, block % 4, z_slots[block // 4], :, h * tile : (h + 1) * tile] = running[order[3, n]]
         for p in range(len(PARTS)):
             for d in (2, 1, 3):
                 x_copy(par, q, d, p).start()
 
     def reduce_x(i, p):
         _, q, par = split(i)
-        for d in (1, 3, 2):
-            x_copy(par, q, d, p).wait()
         start, count = PARTS[p]
+        wait_bytes(from_x.at[par, q, :, pl.ds(start, count)], xr_sem.at[par, q, p])
         for b in range(start, start + count):
             partial[q, b] = (
                 outgoing[q, x, b] + from_x[par, q, 0, b] + from_x[par, q, 2, b]
@@ -242,8 +250,9 @@
     def reduce_z(i):
         step, q, par = split(i)
         reduce_x(i, len(PARTS) - 1)
-        for d in (1, 3, 2):
-            z_copy(par, q, d).wait()
+        wait_bytes(from_z.at[par, q], zr_sem.at[par, q])
+        wait_bytes(partial.at[q, pl.ds(0, 3)], zs_sem.at[q])
+        wait_bytes(outgoing.at[q, pl.ds(0, 3)], xs_sem.at[q])
         value = 0.9 * ((partial[q, 3] + from_z[par, q, 0] + from_z[par, q, 2]) + from_z[par, q, 1])
         rows = pl.ds(pl.multiple_of(q * size, size), size)
 
@@ -446,14 +455,14 @@
             pltpu.VMEM((8, units, classes), f32),
             pltpu.VMEM((2, units, classes), f32),
             dma((PIECES,)),
-            dma((CHUNKS, 7)),
-            dma((2, CHUNKS, 7)),
-            dma((CHUNKS, 4)),
+            dma((CHUNKS,)),
             dma((2, CHUNKS, 4)),
-            dma((CHUNKS, 3, len(PARTS))),
-            dma((2, CHUNKS, 3, len(PARTS))),
-            dma((CHUNKS, 3)),
-            dma((2, CHUNKS, 3)),
+            dma((CHUNKS,)),
+            dma((2, CHUNKS, 4)),
+            dma((CHUNKS,)),
+            dma((2, CHUNKS, len(PARTS))),
+            dma((CHUNKS,)),
+            dma((2, CHUNKS)),
             dma((14,)),
             dma((14,)),
             dma((3,)),

time: 123 us -> 123 us (level)
  no operation moved by 1% of the time
where the time goes in v3:
time: 123 us; the launch traced here: 122 us
  Pallas kernels  121 us (98%)
  between operations  1.29 us (1%)
    pallas_call x1, Pallas kernels, shards(): pl.pallas_call(kernel, out_shape=(jax.ShapeDtypeStruct((classes, width),...  119 us

profile of v3, /device:TPU:1, one launch (start us, length us, event | category | flops | bytes accessed | tf_op | source)
XLA Modules:
  0.0 122.4 jit_solution(4767444511321056234)
XLA Ops:
  1.3 119.4 %shard_map.94 = (f32[64,512]{1,0:T(8,128)}, f32[64,512]{1,0:T(8,128)}, f32[64,64]{1,0:T(8,128)}) custom-call(s32[1,1]{1,0:T(1,128)S(6)} %copy.10.live, s32[1,46]{1,0:T(1,128)} %bitcast.4, s32[1,46]{1,0:T(1,128)} %bitcast.5, s32[1,512]{1,0:T(1,128)} %bitcast.3, f32[64,512]{1,0:T(8,128)} %logits_far.1, f32[64,512]{1,0:T(8,128)} %features_far.1, ...), custom_call_target="tpu_custom_call" | custom-call | flops 4630511616 | bytes 12058624 | tf_op jit(solution)/shard_map/pallas_call | solution.py:421
  120.7 1.7 %shard_map.95 = (f32[64,512]{1,0:T(8,128)}, f32[64,512]{1,0:T(8,128)}, f32[64,64]{1,0:T(8,128)}) custom-call(f32[64,512]{1,0:T(8,128)} %get-tuple-element.6.refs_0_, f32[64,512]{1,0:T(8,128)} %get-tuple-element.7.refs_1_, f32[64,64]{1,0:T(8,128)} %get-tuple-element.8.refs_2_), custom_call_target="tpu_custom_call" | custom-call | tf_op jit(solution)/shard_map/pallas_call | solution.py:487
